TPU v7x, 32 devices: a whole 2x2x4 slice. The times are simulated.
32 devices in a mesh: row: 8 (over y, x, core), col: 4 (over z).
Axes of the slice: x: 2, y: 2, z: 4, core: 2. Of those that a mesh axis runs over, the one named last changes fastest.
Arguments:
- counts: int32 [8192, 8192], P('row', 'col'), may hold values from 0 to 33, as said below
- row_emb: float32 [256, 8192], P('col', 'row'), may hold values from -2 to 2
- col_emb: float32 [256, 8192], P('row', 'col'), may hold values from -2 to 2
- row_accum: float32 [256, 8192], P('col', 'row'), may hold values from 100 to 10000
- col_accum: float32 [256, 8192], P('row', 'col'), may hold values from 100 to 10000
Outputs:
- new_row_emb: float32 [256, 8192], P('col', 'row')
- new_col_emb: float32 [256, 8192], P('row', 'col')
Inputs may be any that keep to these rules, and one draw needn't show every extreme that they name: `counts`: every row word and every column word has a positive count with some partner.
All inputs are finite; a program needn't handle non-finite values.
Results may differ from a plain program's by a relative error of at most 0.0015.
Values may be sent and summed in bfloat16 or wider, within the bound.
A program may use at most 64 MiB of HBM per device.

v0:
```python
import jax
import jax.numpy as jnp
from jax import lax
from jax.sharding import PartitionSpec as P

SWEEPS = 2


def sweep_once(row_emb, col_emb, row_accum, col_accum, positive, target, weight):
    row_half = row_emb.astype(jnp.bfloat16)
    col_half = col_emb.astype(jnp.bfloat16)
    row_block = lax.all_gather(row_half, "col", axis=0, tiled=True)
    col_block = lax.all_gather(col_half, "row", axis=0, tiled=True)
    scores = lax.dot_general(
        row_block, col_block, (((0,), (0,)), ((), ())), preferred_element_type=jnp.float32
    )
    errors = scores - target
    grads = jnp.where(positive, weight * errors, jax.nn.sigmoid(errors)).astype(jnp.bfloat16)
    piece = col_block
    row_grad = lax.psum_scatter(
        lax.dot_general(
            piece, grads, (((1,), (1,)), ((), ())), preferred_element_type=jnp.float32
        ).astype(jnp.bfloat16),
        "col",
        scatter_dimension=0,
        tiled=True,
    ).astype(jnp.float32)
    piece = row_block
    col_grad = lax.psum_scatter(
        jnp.dot(piece, grads, preferred_element_type=jnp.float32).astype(jnp.bfloat16),
        "row",
        scatter_dimension=0,
        tiled=True,
    ).astype(jnp.float32)
    row_accum = row_accum + row_grad * row_grad
    row_emb = row_emb - 0.05 * row_grad / jnp.sqrt(row_accum)
    col_accum = col_accum + col_grad * col_grad
    col_emb = col_emb - 0.05 * col_grad / jnp.sqrt(col_accum)
    return (row_emb, col_emb, row_accum, col_accum)


def on_device(counts, row_emb, col_emb, row_accum, col_accum):
    values = counts.astype(jnp.float32)
    local_rows = jnp.sum(values, axis=1)
    local_cols = jnp.sum(values, axis=0)
    row_marg = lax.psum(local_rows, "col")
    col_marg = lax.psum(local_cols, "row")
    total = lax.psum(jnp.sum(local_rows), ("row", "col"))
    target = (
        jnp.log(jnp.maximum(values, 1.0))
        + jnp.log(total)
        - jnp.log(row_marg)[:, None]
        - jnp.log(col_marg)[None, :]
    )
    weight = 0.1 + 0.25 * jnp.sqrt(values)
    positive = counts > 0
    for sweep in range(SWEEPS):
        row_emb, col_emb, row_accum, col_accum = sweep_once(
            row_emb, col_emb, row_accum, col_accum, positive, target, weight
        )
    return (row_emb, col_emb)


def solution(mesh):
    in_specs = (P("row", "col"), P("col", "row"), P("row", "col"), P("col", "row"), P("row", "col"))
    out_specs = (P("col", "row"), P("row", "col"))
    return jax.shard_map(
        on_device, mesh=mesh, in_specs=in_specs, out_specs=out_specs, check_vma=False
    )
```

profile of v0, /device:TPU:0, one launch (start us, length us, event | category | flops | bytes accessed | tf_op | source)
XLA Modules:
  0.0 283.0 jit_solution(18375166318192286806)
XLA Ops:
  7.2 0.0 copy-start
  7.2 0.0 all-gather.3.cloned.1.call-start
  7.2 1.7 convert_element_type.53
  8.9 0.0 all-gather.3.cloned.1.call-update
  8.9 0.0 reduce-scatter.15.cloned.1.call-start
  8.9 6.9 %convert_reduce_fusion.2 = (f32[]{:T(128)}, f32[1024]{0:T(1024)S(1)}, f32[2048]{0:T(1024)S(1)}) fusion(s32[1024,2048]{1,0:T(8,128)} %param.5), kind=kLoop, calls=%fused_computation.6 | loop fusion | flops 8385535 | bytes 8400900 | tf_op jit(solution)/shard_map/reduce_sum | solution.py:48
  15.9 42.2 %psum.21 = f32[]{:T(128)} all-reduce(f32[]{:T(128)} %get-tuple-element.6), channel_id=1, replica_groups=mesh['row'=8,'col'=4] {'row','col'}, use_global_device_ids=true, to_apply=%region_1.0 | all-reduce | flops 1 | bytes 8 | tf_op jit(solution)/shard_map/psum | solution.py:48
  58.7 10.6 %psum.22 = f32[1024]{0:T(1024)S(1)} all-reduce(f32[1024]{0:T(1024)S(1)} %get-tuple-element.7), channel_id=1, replica_groups=mesh['row'=8,'col'=4] {'col'}, use_global_device_ids=true, to_apply=%region_3.0 | all-reduce | flops 1024 | bytes 8192 | tf_op jit(solution)/shard_map/psum | solution.py:46
  69.4 12.0 %psum.23 = f32[2048]{0:T(1024)S(1)} all-reduce(f32[2048]{0:T(1024)S(1)} %get-tuple-element.8), channel_id=1, replica_groups=mesh['row'=8,'col'=4] {'row'}, use_global_device_ids=true, to_apply=%region_5.0 | all-reduce | flops 2048 | bytes 16384 | tf_op jit(solution)/shard_map/psum | solution.py:47
  81.5 0.0 copy-done
  81.5 16.3 %all_gather.12 = bf16[256,1024]{1,0:T(8,128)(2,1)S(1)} all-gather(bf16[64,1024]{1,0:T(8,128)(2,1)S(1)} %convert_element_type.52), channel_id=1, replica_groups=mesh['row'=8,'col'=4] {'col'}, dimensions={0}, use_global_device_ids=true | all-gather | bytes 655360 | tf_op jit(solution)/shard_map/all_gather | solution.py:12
  97.8 0.0 all-gather.3.cloned.1.call-done
  97.8 12.8 %select_convert_fusion.1 = bf16[1024,2048]{1,0:T(8,128)(2,1)S(1)} fusion(s32[1024,2048]{1,0:T(8,128)} %param.5, bf16[256,1024]{1,0:T(8,128)(2,1)S(1)} %all_gather.12, bf16[256,2048]{1,0:T(8,128)(2,1)} %all-gather.3.cloned.1.call-done, f32[2048]{0:T(1024)S(1)} %log.15, f32[1024]{0:T(1024)S(1)} %log.14, f32[]{:T(128)S(6)} %log.13), kind=kOutput, calls=%fused_computation.1 | convolution fusion | flops 1105199104 | bytes 14168068 | tf_op jit(solution)/shard_map/dot_general | solution.py:14
  110.7 0.0 copy-start.9
  110.7 1.9 copy-done.9
  112.6 0.0 copy-start.6
  112.6 1.3 fusion
  113.9 0.0 copy-start.1
  113.9 0.0 copy-start.3
  114.0 0.0 copy-start.2
  114.0 1.4 copy.33
  115.4 0.0 reduce-scatter.15.cloned.1.call-update
  115.4 0.0 reduce-scatter.13.cloned.1.call-start
  115.5 0.0 copy-done.6
  115.5 3.5 %fusion.1 = bf16[256,1024]{0,1:T(8,128)(2,1)S(1)} fusion(bf16[1024,2048]{1,0:T(8,128)(2,1)} %copy-done.9, bf16[256,2048]{1,0:T(8,128)(2,1)S(1)} %copy-done.6), kind=kOutput, calls=%fused_computation.13 | convolution fusion | flops 1074003968 | bytes 5767168 | tf_op jit(solution)/shard_map/dot_general | solution.py:21
  119.0 1.0 copy.31
  120.0 0.0 reduce-scatter.13.cloned.1.call-update
  120.1 0.0 all-gather.5.cloned.1.call-start
  120.1 29.9 %reduce-scatter.15.cloned.1.call-done = bf16[32,2048]{1,0:T(8,128)(2,1)} async-done(((bf16[256,2048]{1,0:T(8,128)(2,1)}), bf16[32,2048]{1,0:T(8,128)(2,1)}) %reduce-scatter.15.cloned.1.call-update) | async-done | bytes 131088 | tf_op jit(solution)/shard_map/reduce_scatter | solution.py:29
  150.0 0.0 copy-done.1
  150.0 0.0 copy-done.3
  150.0 1.6 fusion.16
  151.6 0.0 all-gather.5.cloned.1.call-update
  151.7 0.0 reduce-scatter.17.cloned.1.call-start
  151.7 22.3 %reduce-scatter.13.cloned.1.call-done = bf16[64,1024]{1,0:T(8,128)(2,1)} async-done(((bf16[256,1024]{1,0:T(8,128)(2,1)}), bf16[64,1024]{1,0:T(8,128)(2,1)}) %reduce-scatter.13.cloned.1.call-update) | async-done | bytes 131088 | tf_op jit(solution)/shard_map/reduce_scatter | solution.py:20
  174.0 0.0 copy-done.2
  174.0 1.0 fusion.17
  174.9 16.0 %all_gather.15 = bf16[256,1024]{1,0:T(8,128)(2,1)S(1)} all-gather(bf16[64,1024]{1,0:T(8,128)(2,1)S(1)} %fusion.17), channel_id=1, replica_groups=mesh['row'=8,'col'=4] {'col'}, dimensions={0}, use_global_device_ids=true | all-gather | bytes 655360 | tf_op jit(solution)/shard_map/all_gather | solution.py:12
  191.0 7.1 %all-gather.5.cloned.1.call-done = bf16[256,2048]{1,0:T(8,128)(2,1)} async-done(((bf16[32,2048]{1,0:T(8,128)(2,1)}), bf16[256,2048]{1,0:T(8,128)(2,1)}) %all-gather.5.cloned.1.call-update) | async-done | bytes 1048592 | tf_op jit(solution)/shard_map/all_gather | solution.py:13
  198.0 0.0 copy-start.7
  198.0 13.2 %select_convert_fusion = bf16[1024,2048]{1,0:T(8,128)(2,1)S(1)} fusion(s32[1024,2048]{1,0:T(8,128)} %param.5, bf16[256,1024]{1,0:T(8,128)(2,1)S(1)} %all_gather.15, bf16[256,2048]{1,0:T(8,128)(2,1)} %all-gather.5.cloned.1.call-done, f32[2048]{0:T(1024)S(1)} %log.15, f32[1024]{0:T(1024)S(1)} %log.14, f32[]{:T(128)S(6)} %log.13), kind=kOutput, calls=%fused_computation | convolution fusion | flops 1105199104 | bytes 14168068 | tf_op jit(solution)/shard_map/dot_general | solution.py:14
  211.2 0.0 copy-start.8
  211.2 1.9 copy-done.8
  213.1 0.0 copy-done.7
  213.1 0.0 copy-start.5
  213.1 0.0 copy-start.4
  213.1 2.1 convolution_convert_fusion.2
  215.2 0.0 reduce-scatter.17.cloned.1.call-update
  215.2 0.0 reduce-scatter.19.cloned.1.call-start
  215.3 4.4 %convolution_convert_fusion = bf16[256,2048]{1,0:T(8,128)(2,1)} fusion(bf16[256,1024]{1,0:T(8,128)(2,1)S(1)} %all_gather.15, bf16[1024,2048]{1,0:T(8,128)(2,1)} %copy-done.8), kind=kOutput, calls=%fused_computation.8 | convolution fusion | flops 1074266112 | bytes 5767168 | tf_op jit(solution)/shard_map/dot_general | solution.py:30
  219.7 0.0 reduce-scatter.19.cloned.1.call-update
  219.7 17.3 %reduce-scatter.17.cloned.1.call-done = bf16[64,1024]{1,0:T(8,128)(2,1)} async-done(((bf16[256,1024]{1,0:T(8,128)(2,1)}), bf16[64,1024]{1,0:T(8,128)(2,1)}) %reduce-scatter.17.cloned.1.call-update) | async-done | bytes 131088 | tf_op jit(solution)/shard_map/reduce_scatter | solution.py:20
  237.1 0.0 copy-done.5
  237.1 1.7 fusion.9
  238.8 35.6 %reduce-scatter.19.cloned.1.call-done = bf16[32,2048]{1,0:T(8,128)(2,1)} async-done(((bf16[256,2048]{1,0:T(8,128)(2,1)}), bf16[32,2048]{1,0:T(8,128)(2,1)}) %reduce-scatter.19.cloned.1.call-update) | async-done | bytes 131088 | tf_op jit(solution)/shard_map/reduce_scatter | solution.py:29
  274.4 0.0 copy-done.4
  274.4 1.7 fusion.13
  (3 shorter events, 0.0 us)
Async XLA Ops:
  7.2 74.3 %copy-start = (f32[64,1024]{1,0:T(8,128)S(1)}, f32[64,1024]{1,0:T(8,128)}, u32[]{:S(2)}) copy-start(f32[64,1024]{1,0:T(8,128)} %param.6) | copy-start | bytes 786436
  7.2 90.6 %all-gather.3.cloned.1.call-start = ((), (), s32[]{:S(2)}) async-start(), calls=%async_computation.4 | async-start | bytes 1179648 | tf_op jit(solution)/shard_map/all_gather | solution.py:13
  8.9 141.1 %reduce-scatter.15.cloned.1.call-start = ((), (), s32[]{:S(2)}) async-start(), calls=%async_computation.7 | async-start | bytes 1179648 | tf_op jit(solution)/shard_map/reduce_scatter | solution.py:29
  110.7 1.9 copy-start.9
  112.6 2.9 %copy-start.6 = (bf16[256,2048]{1,0:T(8,128)(2,1)S(1)}, bf16[256,2048]{1,0:T(8,128)(2,1)}, u32[]{:S(2)}) copy-start(bf16[256,2048]{1,0:T(8,128)(2,1)} %all-gather.3.cloned.1.call-done) | copy-start | bytes 3145732
  113.9 36.1 %copy-start.1 = (f32[32,2048]{1,0:T(8,128)S(1)}, f32[32,2048]{1,0:T(8,128)}, u32[]{:S(2)}) copy-start(f32[32,2048]{1,0:T(8,128)} %param.7) | copy-start | bytes 786436
  113.9 36.1 %copy-start.3 = (f32[32,2048]{1,0:T(8,128)S(1)}, f32[32,2048]{1,0:T(8,128)}, u32[]{:S(2)}) copy-start(f32[32,2048]{1,0:T(8,128)} %param.9) | copy-start | bytes 786436
  114.0 60.0 %copy-start.2 = (f32[64,1024]{1,0:T(8,128)S(1)}, f32[64,1024]{1,0:T(8,128)}, u32[]{:S(2)}) copy-start(f32[64,1024]{1,0:T(8,128)} %param.8) | copy-start | bytes 786436
  115.4 58.5 %reduce-scatter.13.cloned.1.call-start = ((), (), s32[]{:S(2)}) async-start(), calls=%async_computation.6 | async-start | bytes 655360 | tf_op jit(solution)/shard_map/reduce_scatter | solution.py:20
  120.1 78.0 %all-gather.5.cloned.1.call-start = ((), (), s32[]{:S(2)}) async-start(), calls=%async_computation.5 | async-start | bytes 1179648 | tf_op jit(solution)/shard_map/all_gather | solution.py:13
  151.7 85.4 %reduce-scatter.17.cloned.1.call-start = ((), (), s32[]{:S(2)}) async-start(), calls=%async_computation.8 | async-start | bytes 655360 | tf_op jit(solution)/shard_map/reduce_scatter | solution.py:20
  198.0 15.1 %copy-start.7 = (bf16[256,2048]{1,0:T(8,128)(2,1)S(1)}, bf16[256,2048]{1,0:T(8,128)(2,1)}, u32[]{:S(2)}) copy-start(bf16[256,2048]{1,0:T(8,128)(2,1)} %all-gather.5.cloned.1.call-done) | copy-start | bytes 3145732
  211.2 1.9 copy-start.8
  213.1 24.0 %copy-start.5 = (bf16[64,1024]{1,0:T(8,128)(2,1)S(1)}, bf16[64,1024]{1,0:T(8,128)(2,1)}, u32[]{:S(2)}) copy-start(bf16[64,1024]{1,0:T(8,128)(2,1)} %reduce-scatter.13.cloned.1.call-done) | copy-start | bytes 393220
  213.1 61.2 %copy-start.4 = (bf16[32,2048]{1,0:T(8,128)(2,1)S(1)}, bf16[32,2048]{1,0:T(8,128)(2,1)}, u32[]{:S(2)}) copy-start(bf16[32,2048]{1,0:T(8,128)(2,1)} %reduce-scatter.15.cloned.1.call-done) | copy-start | bytes 393220
  215.2 59.1 %reduce-scatter.19.cloned.1.call-start = ((), (), s32[]{:S(2)}) async-start(), calls=%async_computation.9 | async-start | bytes 1179648 | tf_op jit(solution)/shard_map/reduce_scatter | solution.py:29
Sparse Core Ops, SparseCore 0:
  10.5 26.5 all-gather.2
  115.6 34.3 reduce-scatter.14
  152.3 21.6 reduce-scatter.12
  176.3 21.6 all-gather.4
  215.4 21.6 reduce-scatter.16
  240.1 34.2 reduce-scatter.18
where the time goes:
time: 283 us
  waiting for transfers between devices  112 us (40%)
  blocking collectives  97.2 us (34%)
  matrix products  37.4 us (13%)
  between operations  14.9 us (5%)
  other arithmetic  14.7 us (5%)
  local copies, waits for them, and re-layouts  6.33 us (2%)
    reduce_scatter x2, waiting for transfers between devices, sweep_once(): lax.psum_scatter(jnp.dot(piece, grads, preferred_element_type=jnp.float32...  65.4 us
    psum x1, blocking collectives, on_device(): total = lax.psum(jnp.sum(local_rows), ('row', 'col'))  42.2 us
    reduce_scatter x2, waiting for transfers between devices, sweep_once(): lax.psum_scatter(lax.dot_general(piece, grads, (((1,), (1,)), ((), ())),...  39.6 us
    all_gather x2, blocking collectives, sweep_once(): row_block = lax.all_gather(row_half, 'col', axis=0, tiled=True)  32.3 us
    dot_general x2, matrix products, sweep_once(): lax.dot_general(row_block, col_block, (((0,), (0,)), ((), ())), preferred...  26 us
    psum x1, blocking collectives, on_device(): col_marg = lax.psum(local_cols, 'row')  12 us
    psum x1, blocking collectives, on_device(): row_marg = lax.psum(local_rows, 'col')  10.6 us
    all_gather x2, waiting for transfers between devices, sweep_once(): col_block = lax.all_gather(col_half, 'row', axis=0, tiled=True)  7.07 us
  transfers between devices with their start and end apart: 6, of which 5 were waited for; matrix products, arithmetic and copies ran while one was open for 7% of the time, Pallas kernels for 0%

commit v1 on v0

v1 whole, which is shorter than its diff:
```python
import functools

import jax
import jax.numpy as jnp
from jax import lax
from jax.experimental import pallas as pl
from jax.experimental.pallas import tpu as pltpu
from jax.sharding import PartitionSpec as P

SWEEPS = 2
ROW_CHUNKS = 4
COL_CHUNKS = 4
MESH = pl.DeviceIdType.MESH
F32 = jnp.float32
BF16 = jnp.bfloat16


def kernel(
    n_row, n_col, counts_hbm, row_emb_in, col_emb_in, row_acc_in, col_acc_in, row_out, col_out,
    counts, base, weight, grads, row_shift, col_shift, row_stat, col_stat, tot_stat,
    row_blk, col_blk, row_part, col_part, row_recv, col_recv, row_acc, col_acc,
    load_sem, rs_send, rs_recv, cs_send, cs_recv, ts_send, ts_recv,
    rg_send, rg_recv, cg_send, cg_recv, rr_send, rr_recv, cr_send, cr_recv,
):
    me_r, me_c = lax.axis_index("row"), lax.axis_index("col")
    br, bc = counts.shape
    dr, dc = row_emb_in.shape[0], col_emb_in.shape[0]
    d = dr * n_col
    cr, cc = br // ROW_CHUNKS, bc // COL_CHUNKS

    def peer(axis, k):
        return lax.rem(me_r + k, n_row) if axis == "row" else lax.rem(me_c + k, n_col)

    def copy(axis, k, src, dst, send_sem, recv_sem):
        return pltpu.make_async_remote_copy(
            src_ref=src, dst_ref=dst, send_sem=send_sem, recv_sem=recv_sem,
            device_id={axis: peer(axis, k)}, device_id_type=MESH,
        )

    def load(c):
        rows = pl.ds(pl.multiple_of(c * cr, cr), cr)
        return pltpu.make_async_copy(counts_hbm.at[rows, :], counts.at[rows, :], load_sem.at[c])

    def rcols(c):
        return pl.ds(pl.multiple_of(c * cr, cr), cr)

    def ccols(c):
        return pl.ds(pl.multiple_of(c * cc, cc), cc)

    def row_gather(s, c, k):
        own = row_blk.at[s, me_c, :, rcols(c)]
        return copy("col", k, own, own, rg_send.at[s, c, k], rg_recv.at[s, c, me_c])

    def row_gather_in(s, c, k):
        p = peer("col", k)
        slot = row_blk.at[s, p, :, rcols(c)]
        return copy("col", k, slot, slot, rg_send.at[s, c, k], rg_recv.at[s, c, p])

    def col_gather(s, c, k):
        own = col_blk.at[s, me_r, :, ccols(c)]
        return copy("row", k, own, own, cg_send.at[s, c, k], cg_recv.at[s, c, me_r])

    def col_gather_in(s, c, k):
        p = peer("row", k)
        slot = col_blk.at[s, p, :, ccols(c)]
        return copy("row", k, slot, slot, cg_send.at[s, c, k], cg_recv.at[s, c, p])

    def row_reduce(s, c, k):
        return copy(
            "col", k, row_part.at[s, peer("col", k), :, rcols(c)], row_recv.at[s, me_c, :, rcols(c)],
            rr_send.at[s, c, k], rr_recv.at[s, c, me_c],
        )

    def row_reduce_in(s, c, k):
        p = peer("col", k)
        slot = row_recv.at[s, p, :, rcols(c)]
        return copy("col", k, slot, slot, rr_send.at[s, c, k], rr_recv.at[s, c, p])

    def col_reduce(s, c, k):
        return copy(
            "row", k, col_part.at[s, peer("row", k), :, ccols(c)], col_recv.at[s, me_r, :, ccols(c)],
            cr_send.at[s, c, k], cr_recv.at[s, c, me_r],
        )

    def col_reduce_in(s, c, k):
        p = peer("row", k)
        slot = col_recv.at[s, p, :, ccols(c)]
        return copy("row", k, slot, slot, cr_send.at[s, c, k], cr_recv.at[s, c, p])

    def stat(axis, k, ref, me, send, recv):
        own = ref.at[me]
        return copy(axis, k, own, own, send.at[k], recv.at[me])

    def stat_in(axis, k, ref, send, recv):
        p = peer(axis, k)
        return copy(axis, k, ref.at[p], ref.at[p], send.at[k], recv.at[p])

    for c in range(ROW_CHUNKS):
        load(c).start()
    row_blk[0, me_c] = row_emb_in[...].astype(BF16)
    col_blk[0, me_r] = col_emb_in[...].astype(BF16)

    barrier = pltpu.get_barrier_semaphore()
    for k in range(1, n_row):
        pl.semaphore_signal(barrier, inc=1, device_id={"row": peer("row", k)}, device_id_type=MESH)
    for k in range(1, n_col):
        pl.semaphore_signal(barrier, inc=1, device_id={"col": peer("col", k)}, device_id_type=MESH)
    pl.semaphore_wait(barrier, n_row + n_col - 2)

    for c in range(ROW_CHUNKS):
        for k in range(1, n_col):
            row_gather(0, c, k).start()
    for c in range(COL_CHUNKS):
        for k in range(1, n_row):
            col_gather(0, c, k).start()

    def count_chunk(c, sums):
        load(c).wait()
        rows = rcols(c)
        rsum = jnp.zeros((8, cr), F32)
        new = []
        for t in range(COL_CHUNKS):
            cols = pl.ds(t * cc, cc)
            v = counts[rows, cols].astype(F32)
            m = jnp.maximum(v, 1.0)
            base[rows, cols] = jnp.log(m)
            weight[rows, cols] = 0.1 + 0.25 * (v * lax.rsqrt(m))
            h = v.astype(BF16)
            new.append(sums[t] + jnp.dot(jnp.ones((8, cr), BF16), h, preferred_element_type=F32))
            rsum = rsum + lax.dot_general(
                jnp.ones((8, cc), BF16), h, (((1,), (1,)), ((), ())), preferred_element_type=F32
            )
        row_stat[me_c, :, rows] = rsum[0:1, :]
        return tuple(new)

    sums = lax.fori_loop(
        0, ROW_CHUNKS, count_chunk, tuple(jnp.zeros((8, cc), F32) for _ in range(COL_CHUNKS))
    )
    for t in range(COL_CHUNKS):
        col_stat[me_r, :, pl.ds(t * cc, cc)] = sums[t][0:1, :]
    for k in range(1, n_row):
        stat("row", k, col_stat, me_r, cs_send, cs_recv).start()
    for k in range(1, n_col):
        stat("col", k, row_stat, me_c, rs_send, rs_recv).start()
    for k in range(1, n_row):
        stat_in("row", k, col_stat, cs_send, cs_recv).wait_recv()
    col_marg = jnp.sum(col_stat[...], axis=0)
    tot_stat[me_c] = jnp.broadcast_to(jnp.sum(col_marg, axis=1, keepdims=True), (1, 128))
    for k in range(1, n_col):
        stat("col", k, tot_stat, me_c, ts_send, ts_recv).start()
    for k in range(1, n_col):
        stat_in("col", k, row_stat, rs_send, rs_recv).wait_recv()
    log_row = jnp.log(jnp.sum(row_stat[...], axis=0))
    row_shift[...] = jnp.transpose(jnp.broadcast_to(log_row, (128, br)))
    for k in range(1, n_col):
        stat_in("col", k, tot_stat, ts_send, ts_recv).wait_recv()
    log_total = jnp.log(jnp.sum(tot_stat[...], axis=0))
    col_shift[...] = jnp.log(col_marg) - jnp.concatenate([log_total] * (bc // 128), axis=1)

    for s in range(SWEEPS):
        last = s == SWEEPS - 1
        row_emb = row_emb_in if s == 0 else row_out
        col_emb = col_emb_in if s == 0 else col_out
        row_accum = row_acc_in if s == 0 else row_acc
        col_accum = col_acc_in if s == 0 else col_acc

        for c in range(COL_CHUNKS):
            for k in range(1, n_row):
                col_gather_in(s, c, k).wait_recv()

        def grad_chunk(c, carry):
            rows = rcols(c)
            for k in range(1, n_col):
                row_gather_in(s, c, k).wait_recv()
            row_half = row_blk[s, :, :, rows].reshape(d, cr)
            shift = jnp.concatenate([row_shift[rows, :]] * (cc // 128), axis=1)
            row_grad = jnp.zeros((d, cr), F32)
            for t in range(COL_CHUNKS):
                cols = pl.ds(t * cc, cc)
                col_half = col_blk[s, :, :, cols].reshape(d, cc)
                scores = lax.dot_general(
                    row_half, col_half, (((0,), (0,)), ((), ())), preferred_element_type=F32
                )
                errors = scores - (base[rows, cols] - (shift + col_shift[:, cols]))
                w = weight[rows, cols]
                g = jnp.where(w > 0.2, w * errors, 0.5 * jnp.tanh(0.5 * errors) + 0.5).astype(BF16)
                grads[rows, cols] = g
                row_grad = row_grad + lax.dot_general(
                    col_half, g, (((1,), (1,)), ((), ())), preferred_element_type=F32
                )
            part = row_grad.astype(BF16).reshape(n_col, dr, cr)
            row_part[s, :, :, rows] = part
            row_recv[s, me_c, :, rows] = row_part[s, me_c, :, rows]
            for k in range(1, n_col):
                row_reduce(s, c, k).start()
            return carry

        lax.fori_loop(0, ROW_CHUNKS, grad_chunk, 0)

        def col_chunk(c, carry):
            cols = ccols(c)
            col_grad = jnp.dot(
                row_blk[s].reshape(d, br), grads[:, cols], preferred_element_type=F32
            )
            col_part[s, :, :, cols] = col_grad.astype(BF16).reshape(n_row, dc, cc)
            col_recv[s, me_r, :, cols] = col_part[s, me_r, :, cols]
            for k in range(1, n_row):
                col_reduce(s, c, k).start()
            return carry

        lax.fori_loop(0, COL_CHUNKS, col_chunk, 0)

        def row_update(c, carry):
            rows = rcols(c)
            for k in range(1, n_col):
                row_reduce_in(s, c, k).wait_recv()
            g = jnp.sum(row_recv[s, :, :, rows].astype(F32), axis=0)
            a = row_accum[:, rows] + g * g
            e = row_emb[:, rows] - 0.05 * g * lax.rsqrt(a)
            row_out[:, rows] = e
            if not last:
                row_acc[:, rows] = a
                row_blk[s + 1, me_c, :, rows] = e.astype(BF16)
                for k in range(1, n_col):
                    row_gather(s + 1, c, k).start()
            return carry

        def col_update(c, carry):
            cols = ccols(c)
            for k in range(1, n_row):
                col_reduce_in(s, c, k).wait_recv()
            g = jnp.sum(col_recv[s, :, :, cols].astype(F32), axis=0)
            a = col_accum[:, cols] + g * g
            e = col_emb[:, cols] - 0.05 * g * lax.rsqrt(a)
            col_out[:, cols] = e
            if not last:
                col_acc[:, cols] = a
                col_blk[s + 1, me_r, :, cols] = e.astype(BF16)
                for k in range(1, n_row):
                    col_gather(s + 1, c, k).start()
            return carry

        lax.fori_loop(0, ROW_CHUNKS, row_update, 0)
        lax.fori_loop(0, COL_CHUNKS, col_update, 0)

    for k in range(1, n_row):
        stat("row", k, col_stat, me_r, cs_send, cs_recv).wait_send()
    for k in range(1, n_col):
        stat("col", k, row_stat, me_c, rs_send, rs_recv).wait_send()
        stat("col", k, tot_stat, me_c, ts_send, ts_recv).wait_send()
    for s in range(SWEEPS):
        for c in range(ROW_CHUNKS):
            for k in range(1, n_col):
                row_gather(s, c, k).wait_send()
                row_reduce(s, c, k).wait_send()
        for c in range(COL_CHUNKS):
            for k in range(1, n_row):
                col_gather(s, c, k).wait_send()
                col_reduce(s, c, k).wait_send()


def on_device(n_row, n_col, counts, row_emb, col_emb, row_accum, col_accum):
    br, bc = counts.shape
    dr, dc = row_emb.shape[0], col_emb.shape[0]
    dma = pltpu.SemaphoreType.DMA
    vmem = pl.BlockSpec(memory_space=pltpu.VMEM)
    return pl.pallas_call(
        functools.partial(kernel, n_row, n_col),
        out_shape=(
            jax.ShapeDtypeStruct(row_emb.shape, F32),
            jax.ShapeDtypeStruct(col_emb.shape, F32),
        ),
        in_specs=[pl.BlockSpec(memory_space=pl.ANY), vmem, vmem, vmem, vmem],
        out_specs=(vmem, vmem),
        scratch_shapes=[
            pltpu.VMEM((br, bc), jnp.int32),
            pltpu.VMEM((br, bc), F32),
            pltpu.VMEM((br, bc), F32),
            pltpu.VMEM((br, bc), BF16),
            pltpu.VMEM((br, 128), F32),
            pltpu.VMEM((1, bc), F32),
            pltpu.VMEM((n_col, 1, br), F32),
            pltpu.VMEM((n_row, 1, bc), F32),
            pltpu.VMEM((n_col, 1, 128), F32),
            pltpu.VMEM((SWEEPS, n_col, dr, br), BF16),
            pltpu.VMEM((SWEEPS, n_row, dc, bc), BF16),
            pltpu.VMEM((SWEEPS, n_col, dr, br), BF16),
            pltpu.VMEM((SWEEPS, n_row, dc, bc), BF16),
            pltpu.VMEM((SWEEPS, n_col, dr, br), BF16),
            pltpu.VMEM((SWEEPS, n_row, dc, bc), BF16),
            pltpu.VMEM((dr, br), F32),
            pltpu.VMEM((dc, bc), F32),
            dma((ROW_CHUNKS,)),
            dma((n_col,)),
            dma((n_col,)),
            dma((n_row,)),
            dma((n_row,)),
            dma((n_col,)),
            dma((n_col,)),
            dma((SWEEPS, ROW_CHUNKS, n_col)),
            dma((SWEEPS, ROW_CHUNKS, n_col)),
            dma((SWEEPS, COL_CHUNKS, n_row)),
            dma((SWEEPS, COL_CHUNKS, n_row)),
            dma((SWEEPS, ROW_CHUNKS, n_col)),
            dma((SWEEPS, ROW_CHUNKS, n_col)),
            dma((SWEEPS, COL_CHUNKS, n_row)),
            dma((SWEEPS, COL_CHUNKS, n_row)),
        ],
        compiler_params=pltpu.CompilerParams(
            collective_id=0, has_side_effects=True, vmem_limit_bytes=56 * 1024 * 1024
        ),
    )(counts, row_emb, col_emb, row_accum, col_accum)


def solution(mesh):
    in_specs = (P("row", "col"), P("col", "row"), P("row", "col"), P("col", "row"), P("row", "col"))
    out_specs = (P("col", "row"), P("row", "col"))
    return jax.shard_map(
        functools.partial(on_device, mesh.shape["row"], mesh.shape["col"]),
        mesh=mesh, in_specs=in_specs, out_specs=out_specs, check_vma=False,
    )
```

time: 283 us -> 82.3 us (0.29)
  waiting for transfers between devices: 112 us -> 0 us
  blocking collectives: 97.2 us -> 0 us
  Pallas kernels: 0 us -> 78.2 us
  matrix products: 37.4 us -> 0 us
  other arithmetic: 14.7 us -> 0 us
  between operations: 14.9 us -> 0.64 us
  local copies, waits for them, and re-layouts: 6.33 us -> 3.34 us
    reduce_scatter x4 -> x0, waiting for transfers between devices: 105 us -> none  [the longest x2 65.4 us: sweep_once(): lax.psum_scatter(jnp.dot(piece, grads, preferred_element_type=jnp.float32...]
    pallas_call x0 -> x1, Pallas kernels: none -> 78.2 us  [on_device(): pl.pallas_call(functools.partial(kernel, n_row, n_col), out_shape=(jax.Sh...]
    psum x3 -> x0, blocking collectives: 64.8 us -> none  [the longest x1 42.2 us: on_device(): total = lax.psum(jnp.sum(local_rows), ('row', 'col'))]
    dot_general x6 -> x0, matrix products: 37.4 us -> none  [the longest x2 26 us: sweep_once(): lax.dot_general(row_block, col_block, (((0,), (0,)), ((), ())), preferred...]
    all_gather x2 -> x0, blocking collectives: 32.3 us -> none  [sweep_once(): row_block = lax.all_gather(row_half, 'col', axis=0, tiled=True)]
    all_gather x2 -> x0, waiting for transfers between devices: 7.07 us -> none  [sweep_once(): col_block = lax.all_gather(col_half, 'row', axis=0, tiled=True)]
    reduce_sum x1 -> x0, other arithmetic: 6.94 us -> none  [on_device(): total = lax.psum(jnp.sum(local_rows), ('row', 'col'))]
    convert_element_type x4 -> x0, other arithmetic: 4.27 us -> none  [the longest x2 3.28 us: sweep_once(): col_half = col_emb.astype(jnp.bfloat16)]
  transfers between devices with their start and end apart: 6 -> 0, of which waited for: 5 -> 0; matrix products, arithmetic and copies ran while one was open for 7% -> 0% of each run, Pallas kernels for 0% -> 0%
where the time goes in v1:
time: 82.3 us; the launch traced here: 82.1 us
  Pallas kernels  78.2 us (95%)
  local copies, waits for them, and re-layouts  3.34 us (4%)
    pallas_call x1, Pallas kernels, on_device(): pl.pallas_call(functools.partial(kernel, n_row, n_col), out_shape=(jax.Sh...  78.2 us
    unnamed x2, local copies, waits for them, and re-layouts  3.34 us

profile of v1, /device:TPU:0, one launch (start us, length us, event | category | flops | bytes accessed | tf_op | source)
XLA Modules:
  0.0 82.1 jit_solution(18254367003652167025)
XLA Ops:
  0.6 78.2 %shard_map.68 = (f32[64,1024]{1,0:T(8,128)}, f32[32,2048]{1,0:T(8,128)}) custom-call(s32[1024,2048]{1,0:T(8,128)} %counts_hbm.1, f32[64,1024]{1,0:T(8,128)} %row_emb_in.1, f32[32,2048]{1,0:T(8,128)} %col_emb_in.1, f32[64,1024]{1,0:T(8,128)} %row_acc_in.1, f32[32,2048]{1,0:T(8,128)} %col_acc_in.1), custom_call_target="tpu_custom_call" | custom-call | tf_op jit(solution)/shard_map/pallas_call | solution.py:267
  78.8 1.7 %copy.9 = f32[64,1024]{1,0:T(8,128)} copy(f32[64,1024]{1,0:T(8,128)} %get-tuple-element.4) | data formatting | bytes 524288
  80.5 1.7 %copy.10 = f32[32,2048]{1,0:T(8,128)} copy(f32[32,2048]{1,0:T(8,128)} %get-tuple-element.5) | data formatting | bytes 524288

commit v2 on v1

--- a/solution.py
+++ b/solution.py
@@ -18,15 +18,21 @@
 def kernel(
     n_row, n_col, counts_hbm, row_emb_in, col_emb_in, row_acc_in, col_acc_in, row_out, col_out,
     counts, base, weight, grads, row_shift, col_shift, row_stat, col_stat, tot_stat,
-    row_blk, col_blk, row_part, col_part, row_recv, col_recv, row_acc, col_acc,
+    row_blk, col_blk, row_part, col_part, pair_recv, col_sum, row_recv, col_recv, row_acc, col_acc,
     load_sem, rs_send, rs_recv, cs_send, cs_recv, ts_send, ts_recv,
-    rg_send, rg_recv, cg_send, cg_recv, rr_send, rr_recv, cr_send, cr_recv,
+    rg_send, rg_recv, rf_send, cg_send, cg_recv, cf_send, rr_send, rr_recv,
+    pr_send, pr_recv, cr_send, cr_recv,
 ):
     me_r, me_c = lax.axis_index("row"), lax.axis_index("col")
     br, bc = counts.shape
     dr, dc = row_emb_in.shape[0], col_emb_in.shape[0]
     d = dr * n_col
     cr, cc = br // ROW_CHUNKS, bc // COL_CHUNKS
+    chips, side = n_row // 2, lax.rem(me_r, 2)
+    other = 1 - side
+    me_q = lax.div(me_r, 2)
+    sibling = 2 * me_q + other
+    first, end = 0, n_col - 1
 
     def peer(axis, k):
         return lax.rem(me_r + k, n_row) if axis == "row" else lax.rem(me_c + k, n_col)
@@ -56,14 +62,84 @@
         slot = row_blk.at[s, p, :, rcols(c)]
         return copy("col", k, slot, slot, rg_send.at[s, c, k], rg_recv.at[s, c, p])
 
+    def row_far(k):
+        if k == 1:
+            return me_c != end
+        if k == n_col - 1:
+            return me_c != first
+        return None
+
+    def row_gather_all(s, c, start):
+        for k in range(1, n_col):
+            go = row_gather(s, c, k).start if start else row_gather(s, c, k).wait_send
+            if row_far(k) is None:
+                go()
+            else:
+                pl.when(row_far(k))(go)
+
+    def row_pass(s, c, to_end):
+        slot = row_blk.at[s, first if to_end else end, :, rcols(c)]
+        return copy(
+            "col", 1 if to_end else n_col - 1, slot, slot,
+            rf_send.at[s, c, int(to_end)], rg_recv.at[s, c, first if to_end else end],
+        )
+
+    def row_relay(s, c):
+        @pl.when(me_c == end - 1)
+        def _():
+            row_gather_in(s, c, 2).wait_recv()
+            row_pass(s, c, True).start()
+
+        @pl.when(me_c == first + 1)
+        def _():
+            row_gather_in(s, c, n_col - 2).wait_recv()
+            row_pass(s, c, False).start()
+
+    def row_rest(s, c):
+        for k in range(1, n_col):
+            wait = row_gather_in(s, c, k).wait_recv
+            here = None
+            if k == 2:
+                here = me_c != end - 1
+            if k == n_col - 2:
+                here = me_c != first + 1 if here is None else here & (me_c != first + 1)
+            if here is None:
+                wait()
+            else:
+                pl.when(here)(wait)
+
+    def chip(k):
+        return lax.rem(me_q + k, chips)
+
+    def put(p, src, dst, send_sem, recv_sem):
+        return pltpu.make_async_remote_copy(
+            src_ref=src, dst_ref=dst, send_sem=send_sem, recv_sem=recv_sem,
+            device_id={"row": p}, device_id_type=MESH,
+        )
+
     def col_gather(s, c, k):
         own = col_blk.at[s, me_r, :, ccols(c)]
-        return copy("row", k, own, own, cg_send.at[s, c, k], cg_recv.at[s, c, me_r])
-
-    def col_gather_in(s, c, k):
-        p = peer("row", k)
+        p = sibling if k == 0 else 2 * chip(k) + side
+        return put(p, own, own, cg_send.at[s, c, k], cg_recv.at[s, c, me_r])
+
+    def col_gather_in(s, c, k, at):
+        p = 2 * chip(k) + at
         slot = col_blk.at[s, p, :, ccols(c)]
-        return copy("row", k, slot, slot, cg_send.at[s, c, k], cg_recv.at[s, c, p])
+        return put(sibling, slot, slot, cg_send.at[s, c, k], cg_recv.at[s, c, p])
+
+    def col_pass(s, c, k):
+        p = 2 * chip(k) + side
+        slot = col_blk.at[s, p, :, ccols(c)]
+        return put(sibling, slot, slot, cf_send.at[s, c, k], cg_recv.at[s, c, p])
+
+    def col_relay(s, c):
+        for k in range(1, chips):
+            col_gather_in(s, c, k, side).wait_recv()
+            col_pass(s, c, k).start()
+
+    def col_rest(s, c):
+        for k in range(chips):
+            col_gather_in(s, c, k, other).wait_recv()
 
     def row_reduce(s, c, k):
         return copy(
@@ -76,16 +152,21 @@
         slot = row_recv.at[s, p, :, rcols(c)]
         return copy("col", k, slot, slot, rr_send.at[s, c, k], rr_recv.at[s, c, p])
 
+    def pair_reduce(s, c):
+        return put(
+            sibling, col_part.at[s, other, :, :, ccols(c)], pair_recv.at[s, :, :, ccols(c)],
+            pr_send.at[s, c], pr_recv.at[s, c],
+        )
+
     def col_reduce(s, c, k):
-        return copy(
-            "row", k, col_part.at[s, peer("row", k), :, ccols(c)], col_recv.at[s, me_r, :, ccols(c)],
-            cr_send.at[s, c, k], cr_recv.at[s, c, me_r],
+        return put(
+            2 * chip(k) + side, col_sum.at[s, chip(k), :, ccols(c)], col_recv.at[s, me_q, :, ccols(c)],
+            cr_send.at[s, c, k], cr_recv.at[s, c, me_q],
         )
 
     def col_reduce_in(s, c, k):
-        p = peer("row", k)
-        slot = col_recv.at[s, p, :, ccols(c)]
-        return copy("row", k, slot, slot, cr_send.at[s, c, k], cr_recv.at[s, c, p])
+        slot = col_recv.at[s, chip(k), :, ccols(c)]
+        return put(2 * chip(k) + side, slot, slot, cr_send.at[s, c, k], cr_recv.at[s, c, chip(k)])
 
     def stat(axis, k, ref, me, send, recv):
         own = ref.at[me]
@@ -108,10 +189,9 @@
     pl.semaphore_wait(barrier, n_row + n_col - 2)
 
     for c in range(ROW_CHUNKS):
-        for k in range(1, n_col):
-            row_gather(0, c, k).start()
+        row_gather_all(0, c, True)
     for c in range(COL_CHUNKS):
-        for k in range(1, n_row):
+        for k in range(chips):
             col_gather(0, c, k).start()
 
     def count_chunk(c, sums):
@@ -142,12 +222,18 @@
         stat("row", k, col_stat, me_r, cs_send, cs_recv).start()
     for k in range(1, n_col):
         stat("col", k, row_stat, me_c, rs_send, rs_recv).start()
+    for c in range(COL_CHUNKS // 2):
+        col_relay(0, c)
     for k in range(1, n_row):
         stat_in("row", k, col_stat, cs_send, cs_recv).wait_recv()
     col_marg = jnp.sum(col_stat[...], axis=0)
     tot_stat[me_c] = jnp.broadcast_to(jnp.sum(col_marg, axis=1, keepdims=True), (1, 128))
     for k in range(1, n_col):
         stat("col", k, tot_stat, me_c, ts_send, ts_recv).start()
+    for c in range(ROW_CHUNKS):
+        row_relay(0, c)
+    for c in range(COL_CHUNKS // 2, COL_CHUNKS):
+        col_relay(0, c)
     for k in range(1, n_col):
         stat_in("col", k, row_stat, rs_send, rs_recv).wait_recv()
     log_row = jnp.log(jnp.sum(row_stat[...], axis=0))
@@ -165,13 +251,11 @@
         col_accum = col_acc_in if s == 0 else col_acc
 
         for c in range(COL_CHUNKS):
-            for k in range(1, n_row):
-                col_gather_in(s, c, k).wait_recv()
+            col_rest(s, c)
 
         def grad_chunk(c, carry):
             rows = rcols(c)
-            for k in range(1, n_col):
-                row_gather_in(s, c, k).wait_recv()
+            row_rest(s, c)
             row_half = row_blk[s, :, :, rows].reshape(d, cr)
             shift = jnp.concatenate([row_shift[rows, :]] * (cc // 128), axis=1)
             row_grad = jnp.zeros((d, cr), F32)
@@ -202,13 +286,25 @@
             col_grad = jnp.dot(
                 row_blk[s].reshape(d, br), grads[:, cols], preferred_element_type=F32
             )
-            col_part[s, :, :, cols] = col_grad.astype(BF16).reshape(n_row, dc, cc)
-            col_recv[s, me_r, :, cols] = col_part[s, me_r, :, cols]
-            for k in range(1, n_row):
+            part = col_grad.astype(BF16).reshape(chips, 2, dc, cc)
+            for h in range(2):
+                col_part[s, h, :, :, cols] = part[:, h]
+            pair_reduce(s, c).start()
+            return carry
+
+        lax.fori_loop(0, COL_CHUNKS, col_chunk, 0)
+
+        def pair_chunk(c, carry):
+            cols = ccols(c)
+            pair_reduce(s, c).wait_recv()
+            both = col_part[s, side, :, :, cols].astype(F32) + pair_recv[s, :, :, cols].astype(F32)
+            col_sum[s, :, :, cols] = both.astype(BF16)
+            for k in range(1, chips):
                 col_reduce(s, c, k).start()
+            col_recv[s, me_q, :, cols] = col_sum[s, me_q, :, cols]
             return carry
 
-        lax.fori_loop(0, COL_CHUNKS, col_chunk, 0)
+        lax.fori_loop(0, COL_CHUNKS, pair_chunk, 0)
 
         def row_update(c, carry):
             rows = rcols(c)
@@ -221,13 +317,12 @@
             if not last:
                 row_acc[:, rows] = a
                 row_blk[s + 1, me_c, :, rows] = e.astype(BF16)
-                for k in range(1, n_col):
-                    row_gather(s + 1, c, k).start()
+                row_gather_all(s + 1, c, True)
             return carry
 
         def col_update(c, carry):
             cols = ccols(c)
-            for k in range(1, n_row):
+            for k in range(1, chips):
                 col_reduce_in(s, c, k).wait_recv()
             g = jnp.sum(col_recv[s, :, :, cols].astype(F32), axis=0)
             a = col_accum[:, cols] + g * g
@@ -236,12 +331,17 @@
             if not last:
                 col_acc[:, cols] = a
                 col_blk[s + 1, me_r, :, cols] = e.astype(BF16)
-                for k in range(1, n_row):
+                for k in range(chips):
                     col_gather(s + 1, c, k).start()
             return carry
 
         lax.fori_loop(0, ROW_CHUNKS, row_update, 0)
         lax.fori_loop(0, COL_CHUNKS, col_update, 0)
+        if not last:
+            for c in range(ROW_CHUNKS):
+                row_relay(s + 1, c)
+            for c in range(COL_CHUNKS):
+                col_relay(s + 1, c)
 
     for k in range(1, n_row):
         stat("row", k, col_stat, me_r, cs_send, cs_recv).wait_send()
@@ -250,12 +350,17 @@
         stat("col", k, tot_stat, me_c, ts_send, ts_recv).wait_send()
     for s in range(SWEEPS):
         for c in range(ROW_CHUNKS):
+            row_gather_all(s, c, False)
+            pl.when(me_c == end - 1)(row_pass(s, c, True).wait_send)
+            pl.when(me_c == first + 1)(row_pass(s, c, False).wait_send)
             for k in range(1, n_col):
-                row_gather(s, c, k).wait_send()
                 row_reduce(s, c, k).wait_send()
         for c in range(COL_CHUNKS):
-            for k in range(1, n_row):
+            pair_reduce(s, c).wait_send()
+            for k in range(chips):
                 col_gather(s, c, k).wait_send()
+            for k in range(1, chips):
+                col_pass(s, c, k).wait_send()
                 col_reduce(s, c, k).wait_send()
 
 
@@ -285,9 +390,11 @@
             pltpu.VMEM((SWEEPS, n_col, dr, br), BF16),
             pltpu.VMEM((SWEEPS, n_row, dc, bc), BF16),
             pltpu.VMEM((SWEEPS, n_col, dr, br), BF16),
-            pltpu.VMEM((SWEEPS, n_row, dc, bc), BF16),
+            pltpu.VMEM((SWEEPS, 2, n_row // 2, dc, bc), BF16),
+            pltpu.VMEM((SWEEPS, n_row // 2, dc, bc), BF16),
+            pltpu.VMEM((SWEEPS, n_row // 2, dc, bc), BF16),
             pltpu.VMEM((SWEEPS, n_col, dr, br), BF16),
-            pltpu.VMEM((SWEEPS, n_row, dc, bc), BF16),
+            pltpu.VMEM((SWEEPS, n_row // 2, dc, bc), BF16),
             pltpu.VMEM((dr, br), F32),
             pltpu.VMEM((dc, bc), F32),
             dma((ROW_CHUNKS,)),
@@ -299,12 +406,16 @@
             dma((n_col,)),
             dma((SWEEPS, ROW_CHUNKS, n_col)),
             dma((SWEEPS, ROW_CHUNKS, n_col)),
+            dma((SWEEPS, ROW_CHUNKS, 2)),
+            dma((SWEEPS, COL_CHUNKS, n_row // 2)),
             dma((SWEEPS, COL_CHUNKS, n_row)),
-            dma((SWEEPS, COL_CHUNKS, n_row)),
+            dma((SWEEPS, COL_CHUNKS, n_row // 2)),
             dma((SWEEPS, ROW_CHUNKS, n_col)),
             dma((SWEEPS, ROW_CHUNKS, n_col)),
-            dma((SWEEPS, COL_CHUNKS, n_row)),
-            dma((SWEEPS, COL_CHUNKS, n_row)),
+            dma((SWEEPS, COL_CHUNKS)),
+            dma((SWEEPS, COL_CHUNKS)),
+            dma((SWEEPS, COL_CHUNKS, n_row // 2)),
+            dma((SWEEPS, COL_CHUNKS, n_row // 2)),
         ],
         compiler_params=pltpu.CompilerParams(
             collective_id=0, has_side_effects=True, vmem_limit_bytes=56 * 1024 * 1024

time: 82.3 us -> 65.6 us (0.80)
  Pallas kernels: 78.2 us -> 61.4 us
    pallas_call x1, Pallas kernels: 78.2 us -> 61.4 us  [on_device(): pl.pallas_call(functools.partial(kernel, n_row, n_col), out_shape=(jax.Sh...]
where the time goes in v2:
time: 65.6 us; the launch traced here: 65.4 us
  Pallas kernels  61.4 us (94%)
  local copies, waits for them, and re-layouts  3.34 us (5%)
    pallas_call x1, Pallas kernels, on_device(): pl.pallas_call(functools.partial(kernel, n_row, n_col), out_shape=(jax.Sh...  61.4 us
    unnamed x2, local copies, waits for them, and re-layouts  3.34 us

profile of v2, /device:TPU:0, one launch (start us, length us, event | category | flops | bytes accessed | tf_op | source)
XLA Modules:
  0.0 65.4 jit_solution(12744452616503798024)
XLA Ops:
  0.6 61.4 %shard_map.68 = (f32[64,1024]{1,0:T(8,128)}, f32[32,2048]{1,0:T(8,128)}) custom-call(s32[1024,2048]{1,0:T(8,128)} %counts_hbm.1, f32[64,1024]{1,0:T(8,128)} %row_emb_in.1, f32[32,2048]{1,0:T(8,128)} %col_emb_in.1, f32[64,1024]{1,0:T(8,128)} %row_acc_in.1, f32[32,2048]{1,0:T(8,128)} %col_acc_in.1), custom_call_target="tpu_custom_call" | custom-call | tf_op jit(solution)/shard_map/pallas_call | solution.py:372
  62.0 1.7 %copy.9 = f32[64,1024]{1,0:T(8,128)} copy(f32[64,1024]{1,0:T(8,128)} %get-tuple-element.4) | data formatting | bytes 524288
  63.7 1.7 %copy.10 = f32[32,2048]{1,0:T(8,128)} copy(f32[32,2048]{1,0:T(8,128)} %get-tuple-element.5) | data formatting | bytes 524288
